TPU v7x, 256 devices: a whole 4x4x8 slice. The times are simulated.
256 devices in a mesh: dp: 16 (over y, x_hi, core), mp: 16 (over x_lo, z).
Axes of the slice: x: 4 (x_hi: 2, x_lo: 2; x = x_hi * 2 + x_lo), y: 4, z: 8, core: 2. Of those that a mesh axis runs over, the one named last changes fastest.
Arguments:
- activations: bfloat16 [16384, 4096], P('dp', 'mp'), may hold values from -6 to 6
- out_grads: bfloat16 [16384, 512], P(('dp', 'mp')), may hold values from -6 to 6
- doc_slot: int32 [16384], P('dp'), may hold values from 0 to 7
- input_eigenvectors: bfloat16 [4096, 4096], P(None, 'mp'), as said below
- eigen_out: bfloat16 [512, 512], replicated, as said below
- query_tiles: bfloat16 [32, 512, 4096], P(None, 'dp', 'mp'), may hold values from -6 to 6
- query_pick: int32 [16], replicated, may hold values from 0 to 31, as said below
Outputs:
- preconditioned: bfloat16 [4096, 16, 512], P('mp', None, 'dp')
Inputs may be any that keep to these rules, and one draw needn't show every extreme that they name: `doc_slot`: numbers name documents within the row's own group. `query_pick`: 16 different indices, among them 0 and 31, in no particular order. `input_eigenvectors`: Real-valued basis matrix with columns of unequal length. `eigen_out`: Real-valued basis matrix with columns of unequal length.
All inputs are finite; a program needn't handle non-finite values.
Results may differ from a plain program's by a relative error of at most 0.011.
Values may be sent and summed in bfloat16 or wider, within the bound.
A program may use at most 64 MiB of HBM per device.

v0:
```python
import jax
import jax.numpy as jnp
from jax import lax
from jax.sharding import PartitionSpec as P

DOC_G = 8
DAMPING = 0.1


def shards(
    activations, out_grads, doc_slot, input_eigenvectors, eigen_out, query_tiles, query_pick
):
    local_cols = input_eigenvectors.shape[1]
    basis_part = input_eigenvectors
    rotated_in = jnp.dot(
        lax.all_gather(activations, "mp", axis=1, tiled=True),
        basis_part,
        preferred_element_type=jnp.float32,
    ).astype(jnp.bfloat16)
    rotated_out = jnp.dot(
        lax.all_gather(out_grads, "mp", axis=0, tiled=True),
        eigen_out,
        preferred_element_type=jnp.float32,
    ).astype(jnp.bfloat16)
    onehot = (doc_slot[None, :] == jnp.arange(DOC_G, dtype=jnp.int32)[:, None]).astype(jnp.bfloat16)
    masked_entries = onehot[:, :, None] * rotated_out[None]
    doc_grad = jnp.einsum(
        "nre,rk->nek", masked_entries, rotated_in, preferred_element_type=jnp.float32
    )
    partial_sq = jnp.sum(doc_grad * doc_grad, axis=0)
    owner_rows = query_tiles.shape[1]
    summed = lax.psum(partial_sq, "dp")
    owned = lax.dynamic_slice_in_dim(summed, lax.axis_index("dp") * owner_rows, owner_rows, 0)
    eigen_vals = owned / (DOC_G * lax.axis_size("dp"))
    chosen = jnp.take(query_tiles, query_pick, axis=0).astype(jnp.float32)
    rescaled_gradient = (chosen / (eigen_vals[None] + DAMPING)).astype(jnp.bfloat16)
    selected = rescaled_gradient.shape[0]
    flat_tiles = rescaled_gradient.reshape(selected * owner_rows, local_cols)
    basis_part = input_eigenvectors
    final_output = lax.psum_scatter(
        lax.dot_general(
            basis_part, flat_tiles, (((1,), (1,)), ((), ())), preferred_element_type=jnp.float32
        ),
        "mp",
        scatter_dimension=0,
        tiled=True,
    )
    return final_output.reshape(final_output.shape[0], selected, owner_rows).astype(jnp.bfloat16)


def solution(mesh):
    in_specs = (
        P("dp", "mp"),
        P(("dp", "mp"), None),
        P("dp"),
        P(None, "mp"),
        P(),
        P(None, "dp", "mp"),
        P(),
    )
    out_specs = P("mp", None, "dp")
    return jax.shard_map(shards, mesh=mesh, in_specs=in_specs, out_specs=out_specs, check_vma=False)
```

profile of v0, /device:TPU:1, one launch (start us, length us, event | category | flops | bytes accessed | tf_op | source)
XLA Modules:
  0.0 478.1 jit_solution(12855527956758220249)
XLA Ops:
  6.5 0.0 copy-start
  6.5 0.0 all-gather.3.cloned.1.call-start
  6.5 0.7 all-gather.3.cloned.1.call-update
  7.3 0.0 all-gather.5.cloned.1.call-start
  7.3 0.7 all-gather.5.cloned.1.call-update
  8.0 0.0 all-reduce.2.cloned.1.call-start
  8.1 0.7 fusion.8
  8.8 63.0 %all-gather.3.cloned.1.call-done = bf16[1024,512]{1,0:T(8,128)(2,1)} async-done(((bf16[64,512]{1,0:T(8,128)(2,1)}), bf16[1024,512]{1,0:T(8,128)(2,1)}) %all-gather.3.cloned.1.call-update) | async-done | bytes 1048592 | tf_op jit(solution)/shard_map/all_gather | solution.py:21
  71.8 3.2 convolution_convert_fusion
  75.0 0.0 copy-start.2
  75.0 0.0 copy-start.1
  75.0 125.3 %all-gather.5.cloned.1.call-done = bf16[1024,4096]{1,0:T(8,128)(2,1)} async-done(((bf16[1024,256]{1,0:T(8,128)(2,1)}), bf16[1024,4096]{1,0:T(8,128)(2,1)}) %all-gather.5.cloned.1.call-update) | async-done | bytes 8388624 | tf_op jit(solution)/shard_map/all_gather | solution.py:16
  200.3 0.0 copy-done
  200.3 13.3 %multiply_reduce_fusion = f32[512,256]{1,0:T(8,128)} fusion(bf16[1024,512]{0,1:T(8,128)(2,1)} %convolution_convert_fusion, bf16[8,1024]{1,0:T(8,128)(2,1)S(1)} %fusion.8, bf16[1024,4096]{1,0:T(8,128)(2,1)} %all-gather.5.cloned.1.call-done, bf16[4096,256]{1,0:T(8,128)(2,1)S(1)} %copy-done), kind=kOutput, calls=%fused_computation.4 | convolution fusion | flops 4301389824 | bytes 12075008 | tf_op jit(solution)/shard_map/nre,rk->nek/dot_general | solution.py:27
  213.6 0.0 all-reduce.2.cloned.1.call-update
  213.6 0.0 reduce-scatter.2.cloned.1.call-start
  213.7 0.0 copy-done.2
  213.7 0.1 broadcast_in_dim.21
  213.8 0.1 broadcast_in_dim.22
  213.9 0.0 copy-done.1
  213.9 0.6 gather_fusion
  214.4 147.4 %all-reduce.2.cloned.1.call-done = f32[512,256]{1,0:T(8,128)} async-done(((f32[512,256]{1,0:T(8,128)}), f32[512,256]{1,0:T(8,128)}) %all-reduce.2.cloned.1.call-update) | async-done | bytes 524304 | tf_op jit(solution)/shard_map/psum | solution.py:32
  361.8 0.8 multiply_add_fusion
  362.6 0.1 fusion.7
  362.7 4.5 convolution_bitcast_fusion
  367.2 0.0 reduce-scatter.2.cloned.1.call-update
  367.2 102.5 %reduce-scatter.2.cloned.1.call-done = f32[256,512]{0,1:T(8,128)} async-done(((f32[4096,512]{0,1:T(8,128)}), f32[256,512]{0,1:T(8,128)}) %reduce-scatter.2.cloned.1.call-update) | async-done | bytes 524304 | tf_op jit(solution)/shard_map/reduce_scatter | solution.py:40
  469.8 1.8 convert_element_type.32
  (3 shorter events, 0.0 us)
Async XLA Ops:
  6.5 193.7 %copy-start = (bf16[4096,256]{1,0:T(8,128)(2,1)S(1)}, bf16[4096,256]{1,0:T(8,128)(2,1)}, u32[]{:S(2)}) copy-start(bf16[4096,256]{1,0:T(8,128)(2,1)} %param.10) | copy-start | bytes 6291460
  6.5 65.3 %all-gather.3.cloned.1.call-start = ((), (), s32[]{:S(2)}) async-start(), calls=%async_computation.1 | async-start | bytes 1114112 | tf_op jit(solution)/shard_map/all_gather | solution.py:21
  7.3 193.0 %all-gather.5.cloned.1.call-start = ((), (), s32[]{:S(2)}) async-start(), calls=%async_computation.2 | async-start | bytes 8912896 | tf_op jit(solution)/shard_map/all_gather | solution.py:16
  8.0 353.8 %all-reduce.2.cloned.1.call-start = ((), (), s32[]{:S(2)}) async-start(), calls=%async_computation.3 | async-start | bytes 1048576 | tf_op jit(solution)/shard_map/psum | solution.py:32
  75.0 138.7 %copy-start.2 = (s32[16]{0:T(128)S(1)}, s32[16]{0:T(128)}, u32[]{:S(2)}) copy-start(s32[16]{0:T(128)} %param.13) | copy-start | bytes 196
  75.0 138.9 %copy-start.1 = (bf16[32,32,256]{2,1,0:T(8,128)(2,1)S(1)}, bf16[32,32,256]{2,1,0:T(8,128)(2,1)}, u32[]{:S(2)}) copy-start(bf16[32,32,256]{2,1,0:T(8,128)(2,1)} %param.12) | copy-start | bytes 1572868
  213.6 256.2 %reduce-scatter.2.cloned.1.call-start = ((), (), s32[]{:S(2)}) async-start(), calls=%async_computation.4 | async-start | bytes 8912896 | tf_op jit(solution)/shard_map/reduce_scatter | solution.py:40
Sparse Core Ops, SparseCore 0:
  9.1 62.6 all-gather.2
  73.5 126.7 all-gather.4
  213.7 148.0 all-reduce.1
  367.4 102.3 reduce-scatter.1
where the time goes:
time: 478 us
  waiting for transfers between devices  440 us (92%)
  matrix products  21 us (4%)
  between operations  13.2 us (3%)
    psum x1, waiting for transfers between devices, shards(): summed = lax.psum(partial_sq, 'dp')  147 us
    all_gather x1, waiting for transfers between devices, shards(): lax.all_gather(activations, 'mp', axis=1, tiled=True)  125 us
    reduce_scatter x1, waiting for transfers between devices, shards(): lax.psum_scatter(lax.dot_general(basis_part, flat_tiles, (((1,), (1,)), (...  103 us
    all_gather x1, waiting for transfers between devices, shards(): lax.all_gather(out_grads, 'mp', axis=0, tiled=True)  63 us
    dot_general x1, matrix products, shards(): jnp.einsum('nre,rk->nek', masked_entries, rotated_in, preferred_element_t...  13.3 us
  transfers between devices with their start and end apart: 4, of which 4 were waited for; matrix products, arithmetic and copies ran while one was open for 1% of the time, Pallas kernels for 0%

commit v1 on v0

--- a/solution.py
+++ b/solution.py
@@ -18,7 +18,9 @@
         preferred_element_type=jnp.float32,
     ).astype(jnp.bfloat16)
     rotated_out = jnp.dot(
-        lax.all_gather(out_grads, "mp", axis=0, tiled=True),
+        jnp.concatenate(
+            lax.all_to_all(jnp.stack([out_grads] * lax.axis_size("mp")), "mp", 0, 0), axis=0
+        ),
         eigen_out,
         preferred_element_type=jnp.float32,
     ).astype(jnp.bfloat16)

time: 478 us -> 427 us (0.89)
  waiting for transfers between devices: 440 us -> 377 us
  starting transfers between devices: 0.12 us -> 10.1 us
    all_gather x1 -> x0, waiting for transfers between devices: 63 us -> none  [shards(): lax.all_gather(out_grads, 'mp', axis=0, tiled=True)]
    all_gather x1, waiting for transfers between devices: 125 us -> 93.7 us  [shards(): lax.all_gather(activations, 'mp', axis=1, tiled=True)]
    all_to_all x0 -> x1, waiting for transfers between devices: none -> 30.4 us  [shards(): lax.all_to_all(jnp.stack([out_grads] * lax.axis_size('mp')), 'mp', 0, 0)]
    all_to_all x0 -> x1, starting transfers between devices: none -> 10 us  [shards(): lax.all_to_all(jnp.stack([out_grads] * lax.axis_size('mp')), 'mp', 0, 0)]
where the time goes in v1:
time: 427 us
  waiting for transfers between devices  377 us (88%)
  matrix products  20.6 us (5%)
  between operations  13.2 us (3%)
  starting transfers between devices  10.1 us (2%)
    psum x1, waiting for transfers between devices, shards(): summed = lax.psum(partial_sq, 'dp')  149 us
    reduce_scatter x1, waiting for transfers between devices, shards(): lax.psum_scatter(lax.dot_general(basis_part, flat_tiles, (((1,), (1,)), (...  103 us
    all_gather x1, waiting for transfers between devices, shards(): lax.all_gather(activations, 'mp', axis=1, tiled=True)  93.7 us
    all_to_all x1, waiting for transfers between devices, shards(): lax.all_to_all(jnp.stack([out_grads] * lax.axis_size('mp')), 'mp', 0, 0)  30.4 us
    dot_general x1, matrix products, shards(): jnp.einsum('nre,rk->nek', masked_entries, rotated_in, preferred_element_t...  13.3 us
    all_to_all x1, starting transfers between devices, shards(): lax.all_to_all(jnp.stack([out_grads] * lax.axis_size('mp')), 'mp', 0, 0)  10 us
  transfers between devices with their start and end apart: 4, of which 4 were waited for; matrix products, arithmetic and copies ran while one was open for 1% of the time, Pallas kernels for 0%

profile of v1, /device:TPU:1, one launch (start us, length us, event | category | flops | bytes accessed | tf_op | source)
XLA Modules:
  0.0 426.7 jit_solution(4277283915246342543)
XLA Ops:
  6.5 0.0 copy-start
  6.5 0.0 all-gather.2.cloned.1.call-start
  6.5 0.7 all-gather.2.cloned.1.call-update
  7.3 2.0 stack.2
  9.2 10.0 %all-to-all-start = ((bf16[16,64,512]{2,1,0:T(8,128)(2,1)}), bf16[16,64,512]{2,1,0:T(8,128)(2,1)S(1)}, u32[]{:S(2)}, u32[]{:S(2)}) async-start(bf16[16,64,512]{2,1,0:T(8,128)(2,1)} %stack.2), calls=%async_computation | async-start | bytes 2097152 | tf_op jit(solution)/shard_map/all_to_all | solution.py:22
  19.3 0.0 all-reduce.2.cloned.1.call-start
  19.3 0.7 fusion.8
  20.0 30.4 %all-to-all-done = bf16[16,64,512]{2,1,0:T(8,128)(2,1)S(1)} async-done(((bf16[16,64,512]{2,1,0:T(8,128)(2,1)}), bf16[16,64,512]{2,1,0:T(8,128)(2,1)S(1)}, u32[]{:S(2)}, u32[]{:S(2)}) %all-to-all-start) | async-done | bytes 1048608 | tf_op jit(solution)/shard_map/all_to_all | solution.py:22
  50.5 2.8 convolution_convert_fusion
  53.3 0.0 copy-start.2
  53.3 0.0 copy-start.1
  53.3 93.7 %all-gather.2.cloned.1.call-done = bf16[1024,4096]{1,0:T(8,128)(2,1)} async-done(((bf16[1024,256]{1,0:T(8,128)(2,1)}), bf16[1024,4096]{1,0:T(8,128)(2,1)}) %all-gather.2.cloned.1.call-update) | async-done | bytes 8388624 | tf_op jit(solution)/shard_map/all_gather | solution.py:16
  147.1 0.0 copy-done
  147.1 13.3 %multiply_reduce_fusion = f32[512,256]{1,0:T(8,128)} fusion(bf16[1024,512]{0,1:T(8,128)(2,1)} %convolution_convert_fusion, bf16[8,1024]{1,0:T(8,128)(2,1)S(1)} %fusion.8, bf16[1024,4096]{1,0:T(8,128)(2,1)} %all-gather.2.cloned.1.call-done, bf16[4096,256]{1,0:T(8,128)(2,1)S(1)} %copy-done), kind=kOutput, calls=%fused_computation.4 | convolution fusion | flops 4301389824 | bytes 12075008 | tf_op jit(solution)/shard_map/nre,rk->nek/dot_general | solution.py:29
  160.3 0.0 all-reduce.2.cloned.1.call-update
  160.4 0.0 reduce-scatter.2.cloned.1.call-start
  160.4 0.0 copy-done.2
  160.4 0.1 broadcast_in_dim.21
  160.5 0.1 broadcast_in_dim.22
  160.6 0.0 copy-done.1
  160.6 0.6 gather_fusion
  161.2 149.2 %all-reduce.2.cloned.1.call-done = f32[512,256]{1,0:T(8,128)} async-done(((f32[512,256]{1,0:T(8,128)}), f32[512,256]{1,0:T(8,128)}) %all-reduce.2.cloned.1.call-update) | async-done | bytes 524304 | tf_op jit(solution)/shard_map/psum | solution.py:34
  310.4 0.8 multiply_add_fusion
  311.2 0.1 fusion.7
  311.3 4.5 %convolution_bitcast_fusion = f32[4096,512]{0,1:T(8,128)} fusion(bf16[512,256]{1,0:T(8,128)(2,1)S(1)} %fusion.7, bf16[4096,256]{1,0:T(8,128)(2,1)S(1)} %copy-done), kind=kOutput, calls=%fused_computation.3 | convolution fusion | flops 1073741824 | bytes 10747904 | tf_op jit(solution)/shard_map/dot_general | solution.py:43
  315.8 0.0 reduce-scatter.2.cloned.1.call-update
  315.8 102.5 %reduce-scatter.2.cloned.1.call-done = f32[256,512]{0,1:T(8,128)} async-done(((f32[4096,512]{0,1:T(8,128)}), f32[256,512]{0,1:T(8,128)}) %reduce-scatter.2.cloned.1.call-update) | async-done | bytes 524304 | tf_op jit(solution)/shard_map/reduce_scatter | solution.py:42
  418.4 1.8 convert_element_type.32
  (3 shorter events, 0.0 us)
Async XLA Ops:
  6.5 140.5 %copy-start = (bf16[4096,256]{1,0:T(8,128)(2,1)S(1)}, bf16[4096,256]{1,0:T(8,128)(2,1)}, u32[]{:S(2)}) copy-start(bf16[4096,256]{1,0:T(8,128)(2,1)} %param.10) | copy-start | bytes 6291460
  6.5 140.5 %all-gather.2.cloned.1.call-start = ((), (), s32[]{:S(2)}) async-start(), calls=%async_computation.2 | async-start | bytes 8912896 | tf_op jit(solution)/shard_map/all_gather | solution.py:16
  9.2 41.2 %all-to-all-start = ((bf16[16,64,512]{2,1,0:T(8,128)(2,1)}), bf16[16,64,512]{2,1,0:T(8,128)(2,1)S(1)}, u32[]{:S(2)}, u32[]{:S(2)}) async-start(bf16[16,64,512]{2,1,0:T(8,128)(2,1)} %stack.2), calls=%async_computation | async-start | bytes 2097152 | tf_op jit(solution)/shard_map/all_to_all | solution.py:22
  19.3 291.1 %all-reduce.2.cloned.1.call-start = ((), (), s32[]{:S(2)}) async-start(), calls=%async_computation.3 | async-start | bytes 1048576 | tf_op jit(solution)/shard_map/psum | solution.py:34
  53.3 107.1 %copy-start.2 = (s32[16]{0:T(128)S(1)}, s32[16]{0:T(128)}, u32[]{:S(2)}) copy-start(s32[16]{0:T(128)} %param.13) | copy-start | bytes 196
  53.3 107.3 %copy-start.1 = (bf16[32,32,256]{2,1,0:T(8,128)(2,1)S(1)}, bf16[32,32,256]{2,1,0:T(8,128)(2,1)}, u32[]{:S(2)}) copy-start(bf16[32,32,256]{2,1,0:T(8,128)(2,1)} %param.12) | copy-start | bytes 1572868
  160.4 258.0 %reduce-scatter.2.cloned.1.call-start = ((), (), s32[]{:S(2)}) async-start(), calls=%async_computation.4 | async-start | bytes 8912896 | tf_op jit(solution)/shard_map/reduce_scatter | solution.py:42
Sparse Core Ops, SparseCore 0:
  9.1 137.9 all-gather.1
  160.5 149.8 all-reduce.1
  316.0 102.3 reduce-scatter.1

commit v2 on v0

--- a/solution.py
+++ b/solution.py
@@ -29,7 +29,7 @@
     )
     partial_sq = jnp.sum(doc_grad * doc_grad, axis=0)
     owner_rows = query_tiles.shape[1]
-    summed = lax.psum(partial_sq, "dp")
+    summed = jnp.sum(lax.all_gather(partial_sq, "dp"), axis=0)
     owned = lax.dynamic_slice_in_dim(summed, lax.axis_index("dp") * owner_rows, owner_rows, 0)
     eigen_vals = owned / (DOC_G * lax.axis_size("dp"))
     chosen = jnp.take(query_tiles, query_pick, axis=0).astype(jnp.float32)

time: 478 us -> 413 us (0.86)
  waiting for transfers between devices: 440 us -> 371 us
    psum x1 -> x0, waiting for transfers between devices: 147 us -> none  [shards(): summed = lax.psum(partial_sq, 'dp')]
    all_gather x0 -> x1, waiting for transfers between devices: none -> 82.1 us  [shards(): summed = jnp.sum(lax.all_gather(partial_sq, 'dp'), axis=0)]
where the time goes in v2:
time: 413 us; the launch traced here: 412 us
  waiting for transfers between devices  371 us (90%)
  matrix products  21 us (5%)
  between operations  13.2 us (3%)
  other arithmetic  6.61 us (2%)
    all_gather x1, waiting for transfers between devices, shards(): lax.all_gather(activations, 'mp', axis=1, tiled=True)  125 us
    reduce_scatter x1, waiting for transfers between devices, shards(): lax.psum_scatter(lax.dot_general(basis_part, flat_tiles, (((1,), (1,)), (...  98.8 us
    all_gather x1, waiting for transfers between devices, shards(): summed = jnp.sum(lax.all_gather(partial_sq, 'dp'), axis=0)  82.1 us
    all_gather x1, waiting for transfers between devices, shards(): lax.all_gather(out_grads, 'mp', axis=0, tiled=True)  63.1 us
    dot_general x1, matrix products, shards(): jnp.einsum('nre,rk->nek', masked_entries, rotated_in, preferred_element_t...  13.3 us
  transfers between devices with their start and end apart: 4, of which 4 were waited for; matrix products, arithmetic and copies ran while one was open for 1% of the time, Pallas kernels for 0%

profile of v2, /device:TPU:1, one launch (start us, length us, event | category | flops | bytes accessed | tf_op | source)
XLA Modules:
  0.0 412.4 jit_solution(10779319688143455733)
XLA Ops:
  6.5 0.0 copy-start
  6.5 0.0 all-gather.5.cloned.1.call-start
  6.5 0.7 all-gather.5.cloned.1.call-update
  7.3 0.0 all-gather.7.cloned.1.call-start
  7.3 0.7 all-gather.7.cloned.1.call-update
  8.0 0.0 all-gather.9.cloned.1.call-start
  8.1 0.7 fusion.8
  8.7 63.1 %all-gather.5.cloned.1.call-done = bf16[1024,512]{1,0:T(8,128)(2,1)} async-done(((bf16[64,512]{1,0:T(8,128)(2,1)}), bf16[1024,512]{1,0:T(8,128)(2,1)}) %all-gather.5.cloned.1.call-update) | async-done | bytes 1048592 | tf_op jit(solution)/shard_map/all_gather | solution.py:21
  71.8 3.2 convolution_convert_fusion
  75.0 0.0 copy-start.2
  75.0 0.0 copy-start.1
  75.0 125.3 %all-gather.7.cloned.1.call-done = bf16[1024,4096]{1,0:T(8,128)(2,1)} async-done(((bf16[1024,256]{1,0:T(8,128)(2,1)}), bf16[1024,4096]{1,0:T(8,128)(2,1)}) %all-gather.7.cloned.1.call-update) | async-done | bytes 8388624 | tf_op jit(solution)/shard_map/all_gather | solution.py:16
  200.3 0.0 copy-done
  200.3 13.3 %multiply_reduce_fusion = f32[512,256]{1,0:T(8,128)} fusion(bf16[1024,512]{0,1:T(8,128)(2,1)} %convolution_convert_fusion, bf16[8,1024]{1,0:T(8,128)(2,1)S(1)} %fusion.8, bf16[1024,4096]{1,0:T(8,128)(2,1)} %all-gather.7.cloned.1.call-done, bf16[4096,256]{1,0:T(8,128)(2,1)S(1)} %copy-done), kind=kOutput, calls=%fused_computation.4 | convolution fusion | flops 4301389824 | bytes 12075008 | tf_op jit(solution)/shard_map/nre,rk->nek/dot_general | solution.py:27
  213.6 0.0 all-gather.9.cloned.1.call-update
  213.6 0.0 reduce-scatter.2.cloned.1.call-start
  213.7 0.0 copy-done.2
  213.7 0.1 broadcast_in_dim.21
  213.8 0.1 broadcast_in_dim.22
  213.9 0.0 copy-done.1
  213.9 0.6 gather_fusion
  214.4 82.1 %all-gather.9.cloned.1.call-done = f32[8192,256]{1,0:T(8,128)} async-done(((f32[512,256]{1,0:T(8,128)}), f32[8192,256]{1,0:T(8,128)}) %all-gather.9.cloned.1.call-update) | async-done | bytes 8388624 | tf_op jit(solution)/shard_map/all_gather | solution.py:32
  296.6 4.0 reduce_sum.19
  300.6 0.1 fusion.7
  300.7 4.5 %convolution_bitcast_fusion = f32[4096,512]{0,1:T(8,128)} fusion(bf16[512,256]{1,0:T(8,128)(2,1)S(1)} %fusion.7, bf16[4096,256]{1,0:T(8,128)(2,1)S(1)} %copy-done), kind=kOutput, calls=%fused_computation.3 | convolution fusion | flops 1073741824 | bytes 10747904 | tf_op jit(solution)/shard_map/dot_general | solution.py:41
  305.2 0.0 reduce-scatter.2.cloned.1.call-update
  305.3 98.8 %reduce-scatter.2.cloned.1.call-done = f32[256,512]{0,1:T(8,128)} async-done(((f32[4096,512]{0,1:T(8,128)}), f32[256,512]{0,1:T(8,128)}) %reduce-scatter.2.cloned.1.call-update) | async-done | bytes 524304 | tf_op jit(solution)/shard_map/reduce_scatter | solution.py:40
  404.1 1.8 convert_element_type.32
  (4 shorter events, 0.0 us)
Async XLA Ops:
  6.5 193.7 %copy-start = (bf16[4096,256]{1,0:T(8,128)(2,1)S(1)}, bf16[4096,256]{1,0:T(8,128)(2,1)}, u32[]{:S(2)}) copy-start(bf16[4096,256]{1,0:T(8,128)(2,1)} %param.10) | copy-start | bytes 6291460
  6.5 65.3 %all-gather.5.cloned.1.call-start = ((), (), s32[]{:S(2)}) async-start(), calls=%async_computation.1 | async-start | bytes 1114112 | tf_op jit(solution)/shard_map/all_gather | solution.py:21
  7.3 193.0 %all-gather.7.cloned.1.call-start = ((), (), s32[]{:S(2)}) async-start(), calls=%async_computation.2 | async-start | bytes 8912896 | tf_op jit(solution)/shard_map/all_gather | solution.py:16
  8.0 288.6 %all-gather.9.cloned.1.call-start = ((), (), s32[]{:S(2)}) async-start(), calls=%async_computation.4 | async-start | bytes 8912896 | tf_op jit(solution)/shard_map/all_gather | solution.py:32
  75.0 138.7 %copy-start.2 = (s32[16]{0:T(128)S(1)}, s32[16]{0:T(128)}, u32[]{:S(2)}) copy-start(s32[16]{0:T(128)} %param.13) | copy-start | bytes 196
  75.0 138.9 %copy-start.1 = (bf16[32,32,256]{2,1,0:T(8,128)(2,1)S(1)}, bf16[32,32,256]{2,1,0:T(8,128)(2,1)}, u32[]{:S(2)}) copy-start(bf16[32,32,256]{2,1,0:T(8,128)(2,1)} %param.12) | copy-start | bytes 1572868
  213.6 190.5 %reduce-scatter.2.cloned.1.call-start = ((), (), s32[]{:S(2)}) async-start(), calls=%async_computation.3 | async-start | bytes 8912896 | tf_op jit(solution)/shard_map/reduce_scatter | solution.py:40
Sparse Core Ops, SparseCore 0:
  9.1 62.6 all-gather.4
  73.5 126.7 all-gather.6
  213.7 82.7 all-gather.8
  305.4 98.6 reduce-scatter.1
